TPU v7x, 32 devices: a whole 2x2x4 slice. The times are simulated.
32 devices in a mesh: parts: 2 (over x), gx: 4 (over y, core), gy: 4 (over z).
Axes of the slice: x: 2, y: 2, z: 4, core: 2. Of those that a mesh axis runs over, the one named last changes fastest.
Arguments:
- forcing_right_side: float32 [32, 32, 1024], P(('parts', 'gx'), 'gy'), parts along dimension 0, may hold values from -18 to 18
- earlier_warmth: float32 [32, 32, 1024], P(('parts', 'gx'), 'gy'), parts along dimension 0, may hold values from 0 to 2
- matter_condition: int32 [32, 32, 1024], P(('parts', 'gx'), 'gy'), parts along dimension 0, may hold values from 0 to 2
- compressed_slot_number: int32 [32, 32, 1024], P(('parts', 'gx'), 'gy'), parts along dimension 0, may hold values from 0 to 127
- normal_draw_factor: float32 [32, 32, 1024], P(('parts', 'gx'), 'gy'), parts along dimension 0, may hold values from -6 to 6
Outputs:
- solution: float32 [32, 32, 1024], P(('parts', 'gx'), 'gy'), parts along dimension 0
- residual: float32 [32, 32, 1024], P(('parts', 'gx'), 'gy'), parts along dimension 0
There are 2 independent parts, one for each index of `parts`. A program takes and returns all parts, laid end to end along the dimension named above; each array names one. Nothing has to cross between parts.
Inputs may be any that keep to these rules, and one draw needn't show every extreme that they name: `matter_condition`: phase labels the cell as powder, solid or liquid. `compressed_slot_number`: each cell's row of the sketch.
All inputs are finite; a program needn't handle non-finite values.
Results may differ from a plain program's by a relative error of at most 0.0003.
Values sent between devices are 32-bit elements; how exact they have to be, the bound alone decides.
No kernel may reach another device: no remote copies, remote signals or barrier semaphores. Data moves between devices by JAX's collectives and lax.ppermute only.
A program may use at most 64 MiB of HBM per device.

v0:
```python
import jax
import jax.numpy as jnp
from jax import lax
from jax.experimental import pallas as pl
from jax.experimental.pallas import tpu as pltpu
from jax.sharding import PartitionSpec as P

SKETCH = 128
LOW = 32
HIGH = SKETCH // LOW
FIELDS = 3
LANES = 128
epsilon = 1e-06


def traits(warmth, phase):
    powder, solid = phase == 0, phase == 1
    offset = jnp.where(powder, 0.2, jnp.where(solid, 1.0, 0.6))
    return offset * (0.5 + warmth), jnp.where(powder, 1.0, jnp.where(solid, 2.0, 1.5))


def link(first, second):
    total = first + second
    return 2.0 * first * second / jnp.where(total > 0.0, total, 1.0)


def ahead(plane, axis):
    return pltpu.roll(plane, plane.shape[axis] - 1, axis)


def inner_links(cond):
    links = []
    for axis in (0, 1):
        index = lax.broadcasted_iota(jnp.int32, cond.shape, axis)
        links.append(
            jnp.where(index < cond.shape[axis] - 1, link(cond, ahead(cond, axis)), 0.0)
        )
    return links


def inner_flow(field, links):
    total = None
    for axis in (0, 1):
        flow = links[axis] * (field - ahead(field, axis))
        part = flow - pltpu.roll(flow, 1, axis)
        total = part if total is None else total + part
    return total


def apply_inside(images, c_wide, caps):
    results = []
    flow_low = link(c_wide[0], c_wide[1]) * (images[0] - images[1])
    for i in range(1, len(images) - 1):
        image = images[i]
        flow = link(c_wide[i], c_wide[i + 1]) * (image - images[i + 1])
        results.append(
            caps[i - 1] * image + inner_flow(image, inner_links(c_wide[i])) + (flow - flow_low)
        )
        flow_low = flow
    return results


def sketch_rows(fields, draws, slots, chosen, cells_ref):
    rows, depth = draws[0].shape
    for i, draw in enumerate(draws):
        coarse, fine = [], []
        for field in fields:
            weighted = draw * field[i]
            head = weighted.astype(jnp.bfloat16).astype(jnp.float32)
            coarse.append(head)
            fine.append(weighted - head)
        for f, part in enumerate(coarse + coarse[:1] + fine + fine[:1]):
            for t in range(depth // LANES):
                cells_ref[t, pl.ds(i * rows * 8 + f, rows, stride=8), :] = part[
                    :, t * LANES : (t + 1) * LANES
                ]
    low_index = lax.broadcasted_iota(jnp.int32, (LOW, depth), 0)
    low_index = low_index.astype(jnp.float32).astype(jnp.bfloat16)
    high_index = lax.broadcasted_iota(jnp.int32, (HIGH * 8, depth), 0) // 8
    high_index = high_index.astype(jnp.float32).astype(jnp.bfloat16)
    total = jnp.zeros((HIGH * 8, LOW), jnp.float32)
    for i, slot in enumerate(slots):
        low = (slot & (LOW - 1)).astype(jnp.float32)
        high = (slot >> (LOW.bit_length() - 1)).astype(jnp.float32)
        left, right = [], []
        for j in chosen:
            at = pl.ds((i * rows + j) * 8, 8)
            cells = [cells_ref[t, at, :] for t in range(depth // LANES)]
            cells = jnp.concatenate(cells, axis=1)
            cells = jnp.concatenate([cells] * HIGH, axis=0).astype(jnp.bfloat16)
            row_high = jnp.broadcast_to(high[j : j + 1], cells.shape).astype(jnp.bfloat16)
            row_low = jnp.broadcast_to(low[j : j + 1], (LOW, depth)).astype(jnp.bfloat16)
            left.append(jnp.where(row_high == high_index, cells, jnp.zeros_like(cells)))
            right.append(
                jnp.where(row_low == low_index, jnp.ones_like(row_low), jnp.zeros_like(row_low))
            )
        total = total + lax.dot_general(
            jnp.concatenate(left, axis=1),
            jnp.concatenate(right, axis=1),
            (((1,), (1,)), ((), ())),
            preferred_element_type=jnp.float32,
        )
    parts = jnp.concatenate([total[h * 8 : h * 8 + 8] for h in range(HIGH)], axis=1)
    return parts + pltpu.roll(parts, 4, 0)


def first_kernel(
    b_hbm, warmth_hbm, phase_hbm, b_ref, cond_ref, cap_ref, inner_ref, first_ref, second_ref,
    warmth_ref, phase_ref, arrived,
):
    copies = [
        pltpu.make_async_copy(source, target, arrived.at[k])
        for k, (source, target) in enumerate(
            ((b_hbm, b_ref), (warmth_hbm, warmth_ref), (phase_hbm, phase_ref))
        )
    ]
    for copy in copies:
        copy.start()
    for copy in copies:
        copy.wait()
    planes = b_ref.shape[0]
    images, conds = [], []
    for i in range(planes):
        cond, cap = traits(warmth_ref[i], phase_ref[i])
        cap_ref[i] = cap
        cond_ref[i] = cond
        field = b_ref[i]
        image = cap * field + inner_flow(field, inner_links(cond))
        if i:
            flow = link(conds[-1], cond) * (b_ref[i - 1] - field)
            images[-1] = images[-1] + flow
            image = image - flow
        conds.append(cond)
        images.append(image)
    for i in range(planes):
        inner_ref[i] = images[i]
    for k, low, high in (
        (0, images[0], images[-1]),
        (1, b_ref[0], b_ref[planes - 1]),
        (2, conds[0], conds[-1]),
    ):
        first_ref[k], second_ref[k] = by_turn(low, high, "gx")


def by_turn(low, high, axis):
    odd = lax.axis_index(axis) % 2 == 1
    return jnp.where(odd, low, high), jnp.where(odd, high, low)


def has_beside(axis):
    at = lax.axis_index(axis)
    return at > 0, at < lax.axis_size(axis) - 1


def second_kernel(
    b_ref, cond_ref, inner_ref, got_first_ref, got_second_ref, wide_ref, beside_ref, first_ref,
    second_ref,
):
    planes, rows = b_ref.shape[0], b_ref.shape[1]
    (image_low, image_high), (b_low, b_high), (c_low, c_high) = (
        by_turn(got_first_ref[k], got_second_ref[k], "gx") for k in range(3)
    )
    below, above = has_beside("gx")
    c_low, c_high = jnp.where(below, c_low, 0.0), jnp.where(above, c_high, 0.0)
    low_flow = link(c_low, cond_ref[0]) * (b_low - b_ref[0])
    high_flow = link(cond_ref[planes - 1], c_high) * (b_ref[planes - 1] - b_high)
    images = [image_low + low_flow] + [inner_ref[i] for i in range(planes)]
    images.append(image_high - high_flow)
    images[1] = images[1] - low_flow
    images[planes] = images[planes] + high_flow
    for i in range(planes + 2):
        wide_ref[i] = images[i]
    for k, plane in enumerate((b_low, b_high, c_low, c_high)):
        beside_ref[k] = plane
    lines = images[1:-1] + [b_low] + [b_ref[i] for i in range(planes)] + [b_high, c_low]
    lines += [cond_ref[i] for i in range(planes)] + [c_high]
    for k, plane in enumerate(lines):
        low, high = by_turn(plane[:1], plane[rows - 1 :], "gy")
        first_ref[k : k + 1] = low
        second_ref[k : k + 1] = high


def reached(rows):
    others = [j for j in range(rows) if 2 <= j < rows - 2]
    return [j for j in range(rows) if j not in others], others


def widened(ref, beside_ref, which):
    inner = [ref[i] for i in range(ref.shape[0])]
    return [beside_ref[which]] + inner + [beside_ref[which + 1]]


def inside_kernel(
    b_ref, cond_ref, cap_ref, slot_ref, draw_ref, wide_ref, beside_ref, sketch_ref,
    cells_ref,
):
    planes = range(b_ref.shape[0])
    images = [wide_ref[i] for i in range(wide_ref.shape[0])]
    c_wide = widened(cond_ref, beside_ref, 2)
    twice = apply_inside(images, c_wide, [cap_ref[i] for i in planes])
    sketch_ref[...] = sketch_rows(
        [[b_ref[i] for i in planes], images[1:-1], twice],
        [draw_ref[i] for i in planes],
        [slot_ref[i] for i in planes],
        reached(b_ref.shape[1])[1],
        cells_ref,
    )


def third_kernel(
    b_ref, cond_ref, cap_ref, slot_ref, draw_ref, wide_ref, beside_ref, got_first_ref,
    got_second_ref, inside_ref, image_ref, twice_ref, sketch_ref, cells_ref,
):
    planes, rows, depth = b_ref.shape
    index = lax.broadcasted_iota(jnp.int32, (rows, depth), 0)
    b_wide = widened(b_ref, beside_ref, 0)
    c_wide = widened(cond_ref, beside_ref, 2)
    below, above = has_beside("gy")
    at_low = (index == 0) & below
    at_high = (index == rows - 1) & above
    lines = by_turn(got_first_ref[...], got_second_ref[...], "gy")
    images, beside = [], []
    for i in range(planes + 2):
        image = wide_ref[i]
        pairs = []
        for line, mask in zip(lines, (at_low, at_high)):
            at = planes + i
            b_side = jnp.broadcast_to(line[at : at + 1], (rows, depth))
            at = 2 * planes + 2 + i
            c_side = jnp.broadcast_to(line[at : at + 1], (rows, depth))
            conductance = jnp.where(mask, link(c_wide[i], c_side), 0.0)
            flow = conductance * (b_wide[i] - b_side)
            image = image + flow
            if 0 < i <= planes:
                beyond = jnp.broadcast_to(line[i - 1 : i], (rows, depth))
                pairs.append((conductance, beyond - flow))
        images.append(image)
        beside.append(pairs)
    twice = apply_inside(images, c_wide, [cap_ref[i] for i in range(planes)])
    for i in range(planes):
        for conductance, value in beside[i + 1]:
            twice[i] = twice[i] + conductance * (images[i + 1] - value)
        image_ref[i] = images[i + 1]
        twice_ref[i] = twice[i]
    sketch = inside_ref[...] + sketch_rows(
        [b_wide[1:-1], images[1:-1], twice],
        [draw_ref[i] for i in range(planes)],
        [slot_ref[i] for i in range(planes)],
        reached(rows)[0],
        cells_ref,
    )
    sketch_ref[...] = sketch[: FIELDS + 1]


def last_kernel(sketch_ref, b_ref, image_ref, twice_ref, solution_ref, residual_ref):
    sketches = jnp.sum(sketch_ref[...], axis=0)

    def inner(first, second):
        return jnp.sum(first * second, axis=1, keepdims=True)

    s0, s1, s2 = (sketches[i : i + 1] for i in range(FIELDS))
    beta = jnp.sqrt(inner(s0, s0) + epsilon)
    q0 = s0 / beta
    p0 = s1 / beta
    h00 = inner(q0, p0)
    t0 = p0 - h00 * q0
    n0 = jnp.sqrt(inner(t0, t0) + epsilon)
    q1 = t0 / n0
    p1 = (s2 / beta - h00 * p0) / n0
    h01 = inner(q0, p1)
    h11 = inner(q1, p1)
    t1 = p1 - h01 * q0 - h11 * q1
    n1 = jnp.sqrt(inner(t1, t1) + epsilon)
    l00 = jnp.sqrt(h00 * h00 + n0 * n0)
    l10 = (h00 * h01 + n0 * h11) / l00
    l11 = jnp.sqrt(h01 * h01 + h11 * h11 + n1 * n1 - l10 * l10)
    z0 = beta * h00 / l00
    z1 = (beta * h01 - l10 * z0) / l11
    y1 = z1 / l11
    y0 = (z0 - l10 * y1) / l00
    c1 = y1 / (beta * n0)
    c0 = y0 / beta - h00 * c1
    for i in range(b_ref.shape[0]):
        b, image = b_ref[i], image_ref[i]
        solution_ref[i] = c0 * b + c1 * image
        residual_ref[i] = b - c0 * image - c1 * twice_ref[i]


def call(kernel, shapes, *operands, scratch=(), inputs=pltpu.VMEM, flops=0):
    return pl.pallas_call(
        kernel,
        out_shape=[jax.ShapeDtypeStruct(shape, jnp.float32) for shape in shapes],
        in_specs=[pl.BlockSpec(memory_space=inputs)] * len(operands),
        out_specs=[pl.BlockSpec(memory_space=pltpu.VMEM)] * len(shapes),
        scratch_shapes=scratch,
        compiler_params=pltpu.CompilerParams(vmem_limit_bytes=48 * 1024 * 1024),
        cost_estimate=pl.CostEstimate(flops=flops, bytes_accessed=0, transcendentals=0),
    )(*operands)


def swap(first, second, axis):
    count = lax.axis_size(axis)
    turns = []
    for array, start in ((first, 0), (second, 1)):
        pairs = [(i, (i + 1) % count) for i in range(start, count, 2)]
        turns.append(lax.ppermute(array, axis, pairs + [(j, i) for i, j in pairs]))
    return turns


def everyones(sketch):
    count = lax.axis_size("gx") * lax.axis_size("gy")
    copies = jnp.broadcast_to(sketch[None], (count,) + sketch.shape)
    return lax.all_to_all(copies, ("gx", "gy"), 0, 0)


def body(b, warmth, phase, slots, draw):
    planes, rows, depth = b.shape
    block, plane, wide = b.shape, (3, rows, depth), (planes + 2, rows, depth)
    line, table = (3 * planes + 4, depth), (8, SKETCH)
    cells = pltpu.VMEM((depth // LANES, planes * rows * 8, LANES), jnp.float32)
    work = b.size * SKETCH * 6
    b, cond, cap, inner, first, second = call(
        first_kernel,
        [block, block, block, block, plane, plane],
        *(pltpu.with_memory_space_constraint(x, pltpu.HBM) for x in (b, warmth, phase)),
        scratch=[
            pltpu.VMEM(block, warmth.dtype),
            pltpu.VMEM(block, phase.dtype),
            pltpu.SemaphoreType.DMA((3,)),
        ],
        inputs=pltpu.HBM,
    )
    image_wide, beside, first, second = call(
        second_kernel,
        [wide, (4, rows, depth), line, line],
        b, cond, inner, *swap(first, second, "gx"),
    )
    got = swap(first, second, "gy")
    (inside,) = call(
        inside_kernel,
        [table],
        b, cond, cap, slots, draw, image_wide, beside,
        scratch=[cells],
        flops=work,
    )
    image, twice, sketch = call(
        third_kernel,
        [block, block, (FIELDS + 1, SKETCH)],
        b, cond, cap, slots, draw, image_wide, beside, *got, inside,
        scratch=[cells],
        flops=work,
    )
    return tuple(call(last_kernel, [block, block], everyones(sketch), b, image, twice))


def solution(mesh):
    spec = P(("parts", "gx"), "gy", None)
    return jax.shard_map(
        body, mesh=mesh, in_specs=(spec,) * 5, out_specs=(spec,) * 2, check_vma=False
    )
```

profile of v0, /device:TPU:0, one launch (start us, length us, event | category | flops | bytes accessed | tf_op | source)
XLA Modules:
  0.0 29.4 jit_solution(7774293455520162021)
XLA Ops:
  0.6 1.3 %shard_map.68 = (f32[4,8,1024]{2,1,0:T(8,128)S(1)}, f32[4,8,1024]{2,1,0:T(8,128)S(1)}, f32[4,8,1024]{2,1,0:T(8,128)S(1)}, f32[4,8,1024]{2,1,0:T(8,128)S(1)}, f32...) custom-call(f32[4,8,1024]{2,1,0:T(8,128)} %b_hbm.1, f32[4,8,1024]{2,1,0:T(8,128)} %warmth_hbm.1, s32[4,8,1024]{2,1,0:T(8,128)} %phase_hbm.1), custom_call_target="tpu_custom_call" | custom-call | tf_op jit(solution)/shard_map/pallas_call | solution.py:290
  1.9 0.5 %collective-permute-start = (f32[3,8,1024]{2,1,0:T(8,128)S(1)}, f32[3,8,1024]{2,1,0:T(8,128)S(1)}, u32[]{:S(2)}, u32[]{:S(2)}) collective-permute-start(f32[3,8,1024]{2,1,0:T(8,128)S(1)} %get-tuple-element.19), channel_id=1, source_target_pairs={{0,4},{8,12},{4,0},{12,8},{1,5},{9,13},{5,1},{13,9},{2,6},{10,14},... | collective-permute-start | bytes 294920 | tf_op jit(solution)/shard_map/ppermute | solution.py:306
  2.5 2.6 %collective-permute-start.1 = (f32[3,8,1024]{2,1,0:T(8,128)S(1)}, f32[3,8,1024]{2,1,0:T(8,128)S(1)}, u32[]{:S(2)}, u32[]{:S(2)}) collective-permute-start(f32[3,8,1024]{2,1,0:T(8,128)S(1)} %get-tuple-element.20), channel_id=1, source_target_pairs={{4,8},{12,0},{8,4},{0,12},{5,9},{13,1},{9,5},{1,13},{6,10},{14,2},... | collective-permute-start | bytes 294920 | tf_op jit(solution)/shard_map/ppermute | solution.py:306
  5.1 0.0 collective-permute-done.got_first_ref
  5.1 3.1 %collective-permute-done.1.got_second_ref = f32[3,8,1024]{2,1,0:T(8,128)S(1)} collective-permute-done((f32[3,8,1024]{2,1,0:T(8,128)S(1)}, f32[3,8,1024]{2,1,0:T(8,128)S(1)}, u32[]{:S(2)}, u32[]{:S(2)}) %collective-permute-start.1) | collective-permute-done | bytes 98336 | tf_op jit(solution)/shard_map/ppermute | solution.py:306
  8.2 0.0 copy-start
  8.2 0.0 copy-start.1
  8.2 0.2 shard_map.69
  8.4 1.6 %collective-permute-start.2 = (f32[16,1024]{1,0:T(8,128)S(1)}, f32[16,1024]{1,0:T(8,128)S(1)}, u32[]{:S(2)}, u32[]{:S(2)}) collective-permute-start(f32[16,1024]{1,0:T(8,128)S(1)} %get-tuple-element.23), channel_id=1, source_target_pairs={{0,1},{2,3},{1,0},{3,2},{4,5},{6,7},{5,4},{7,6},{8,9},{10,11},{9,8... | collective-permute-start | bytes 196616 | tf_op jit(solution)/shard_map/ppermute | solution.py:306
  9.9 2.5 %collective-permute-start.3 = (f32[16,1024]{1,0:T(8,128)S(1)}, f32[16,1024]{1,0:T(8,128)S(1)}, u32[]{:S(2)}, u32[]{:S(2)}) collective-permute-start(f32[16,1024]{1,0:T(8,128)S(1)} %get-tuple-element.24), channel_id=1, source_target_pairs={{1,2},{3,0},{2,1},{0,3},{5,6},{7,4},{6,5},{4,7},{9,10},{11,8},{10,... | collective-permute-start | bytes 196616 | tf_op jit(solution)/shard_map/ppermute | solution.py:306
  12.4 0.0 copy-done
  12.4 0.0 copy-done.1
  12.4 0.8 %shard_map.70.inside_ref = f32[8,128]{1,0:T(8,128)S(1)} custom-call(f32[4,8,1024]{2,1,0:T(8,128)S(1)} %get-tuple-element.15.b_ref, f32[4,8,1024]{2,1,0:T(8,128)S(1)} %get-tuple-element.16.cond_ref, f32[4,8,1024]{2,1,0:T(8,128)S(1)} %get-tuple-element.17.cap_ref, s32[4,8,1024]{2,1,0:T(8,128)S(1)} %copy-done, f32[4,8,1024]{2,1,0:T(8,128)S(1)} %copy-done.1, ...), custom_call_target="tpu_custom_call" | custom-call | flops 25165824 | tf_op jit(solution)/shard_map/pallas_call | solution.py:290
  13.2 0.0 collective-permute-done.2.got_first_ref
  13.2 3.0 %collective-permute-done.3.got_second_ref = f32[16,1024]{1,0:T(8,128)S(1)} collective-permute-done((f32[16,1024]{1,0:T(8,128)S(1)}, f32[16,1024]{1,0:T(8,128)S(1)}, u32[]{:S(2)}, u32[]{:S(2)}) %collective-permute-start.3) | collective-permute-done | bytes 65568 | tf_op jit(solution)/shard_map/ppermute | solution.py:306
  16.2 1.0 %shard_map.71 = (f32[4,8,1024]{2,1,0:T(8,128)S(1)}, f32[4,8,1024]{2,1,0:T(8,128)S(1)}, f32[4,128]{1,0:T(4,128)S(1)}) custom-call(f32[4,8,1024]{2,1,0:T(8,128)S(1)} %get-tuple-element.15.b_ref, f32[4,8,1024]{2,1,0:T(8,128)S(1)} %get-tuple-element.16.cond_ref, f32[4,8,1024]{2,1,0:T(8,128)S(1)} %get-tuple-element.17.cap_ref, s32[4,8,1024]{2,1,0:T(8,128)S(1)} %copy-done, ...), custom_call_target="tpu_custom_call" | custom-call | flops 25165824 | tf_op jit(solution)/shard_map/pallas_call | solution.py:290
  17.2 11.0 %all_to_all.5.sketch_ref = f32[16,4,128]{2,1,0:T(4,128)S(1)} all-to-all(f32[16,4,128]{2,1,0:T(4,128)S(1)} %broadcast_in_dim.2), channel_id=1, replica_groups=mesh['parts'=2,'gx'=4,'gy'=4] {'gx','gy'}, dimensions={0} | all-to-all | bytes 65536 | tf_op jit(solution)/shard_map/all_to_all | solution.py:313
  28.2 1.2 %shard_map.72 = (f32[4,8,1024]{2,1,0:T(8,128)}, f32[4,8,1024]{2,1,0:T(8,128)}) custom-call(f32[16,4,128]{2,1,0:T(4,128)S(1)} %all_to_all.5.sketch_ref, f32[4,8,1024]{2,1,0:T(8,128)S(1)} %get-tuple-element.15.b_ref, f32[4,8,1024]{2,1,0:T(8,128)S(1)} %get-tuple-element.26.image_ref, f32[4,8,1024]{2,1,0:T(8,128)S(1)} %get-tuple-element.27.twice_ref), custom_call_target="tpu_custom_call" | custom-call | tf_op jit(solution)/shard_map/pallas_call | solution.py:290
  (1 shorter events, 0.0 us)
Async XLA Ops:
  1.9 3.2 %collective-permute-start = (f32[3,8,1024]{2,1,0:T(8,128)S(1)}, f32[3,8,1024]{2,1,0:T(8,128)S(1)}, u32[]{:S(2)}, u32[]{:S(2)}) collective-permute-start(f32[3,8,1024]{2,1,0:T(8,128)S(1)} %get-tuple-element.19), channel_id=1, source_target_pairs={{0,4},{8,12},{4,0},{12,8},{1,5},{9,13},{5,1},{13,9},{2,6},{10,14},... | collective-permute-start | bytes 294920 | tf_op jit(solution)/shard_map/ppermute | solution.py:306
  2.5 5.7 %collective-permute-start.1 = (f32[3,8,1024]{2,1,0:T(8,128)S(1)}, f32[3,8,1024]{2,1,0:T(8,128)S(1)}, u32[]{:S(2)}, u32[]{:S(2)}) collective-permute-start(f32[3,8,1024]{2,1,0:T(8,128)S(1)} %get-tuple-element.20), channel_id=1, source_target_pairs={{4,8},{12,0},{8,4},{0,12},{5,9},{13,1},{9,5},{1,13},{6,10},{14,2},... | collective-permute-start | bytes 294920 | tf_op jit(solution)/shard_map/ppermute | solution.py:306
  8.2 4.2 %copy-start = (s32[4,8,1024]{2,1,0:T(8,128)S(1)}, s32[4,8,1024]{2,1,0:T(8,128)}, u32[]{:S(2)}) copy-start(s32[4,8,1024]{2,1,0:T(8,128)} %slot_ref.3) | copy-start | bytes 393220
  8.2 4.2 %copy-start.1 = (f32[4,8,1024]{2,1,0:T(8,128)S(1)}, f32[4,8,1024]{2,1,0:T(8,128)}, u32[]{:S(2)}) copy-start(f32[4,8,1024]{2,1,0:T(8,128)} %draw_ref.3) | copy-start | bytes 393220
  8.4 4.9 %collective-permute-start.2 = (f32[16,1024]{1,0:T(8,128)S(1)}, f32[16,1024]{1,0:T(8,128)S(1)}, u32[]{:S(2)}, u32[]{:S(2)}) collective-permute-start(f32[16,1024]{1,0:T(8,128)S(1)} %get-tuple-element.23), channel_id=1, source_target_pairs={{0,1},{2,3},{1,0},{3,2},{4,5},{6,7},{5,4},{7,6},{8,9},{10,11},{9,8... | collective-permute-start | bytes 196616 | tf_op jit(solution)/shard_map/ppermute | solution.py:306
  9.9 6.3 %collective-permute-start.3 = (f32[16,1024]{1,0:T(8,128)S(1)}, f32[16,1024]{1,0:T(8,128)S(1)}, u32[]{:S(2)}, u32[]{:S(2)}) collective-permute-start(f32[16,1024]{1,0:T(8,128)S(1)} %get-tuple-element.24), channel_id=1, source_target_pairs={{1,2},{3,0},{2,1},{0,3},{5,6},{7,4},{6,5},{4,7},{9,10},{11,8},{10,... | collective-permute-start | bytes 196616 | tf_op jit(solution)/shard_map/ppermute | solution.py:306
where the time goes:
time: 29.6 us; the launch traced here: 29.4 us
  blocking collectives  11 us (37%)
  starting transfers between devices  7.19 us (24%)
  waiting for transfers between devices  6.03 us (20%)
  Pallas kernels  4.58 us (15%)
  between operations  0.66 us (2%)
    all_to_all x1, blocking collectives, everyones(): return lax.all_to_all(copies, ('gx', 'gy'), 0, 0)  11 us
    ppermute x4, starting transfers between devices, swap(): turns.append(lax.ppermute(array, axis, pairs + [(j, i) for i, j in pairs]))  7.19 us
    ppermute x4, waiting for transfers between devices, swap(): turns.append(lax.ppermute(array, axis, pairs + [(j, i) for i, j in pairs]))  6.03 us
    pallas_call x5, Pallas kernels, call(): pl.pallas_call(kernel, out_shape=[jax.ShapeDtypeStruct(shape, jnp.float32...  4.58 us
  transfers between devices with their start and end apart: 4, of which 2 were waited for; matrix products, arithmetic and copies ran while one was open for 0% of the time, Pallas kernels for 3%

commit v1 on v0

--- a/solution.py
+++ b/solution.py
@@ -139,12 +139,20 @@
         (1, b_ref[0], b_ref[planes - 1]),
         (2, conds[0], conds[-1]),
     ):
-        first_ref[k], second_ref[k] = by_turn(low, high, "gx")
-
-
-def by_turn(low, high, axis):
-    odd = lax.axis_index(axis) % 2 == 1
+        first_ref[k], second_ref[k] = to_send(low, high, "gx")
+
+
+ACROSS = {"gx": "gy", "gy": "gx"}
+
+
+def to_send(low, high, axis):
+    odd = lax.axis_index(ACROSS[axis]) % 2 == 1
     return jnp.where(odd, low, high), jnp.where(odd, high, low)
+
+
+def from_beside(first, second, axis):
+    odd = lax.axis_index(ACROSS[axis]) % 2 == 1
+    return jnp.where(odd, second, first), jnp.where(odd, first, second)
 
 
 def has_beside(axis):
@@ -158,7 +166,7 @@
 ):
     planes, rows = b_ref.shape[0], b_ref.shape[1]
     (image_low, image_high), (b_low, b_high), (c_low, c_high) = (
-        by_turn(got_first_ref[k], got_second_ref[k], "gx") for k in range(3)
+        from_beside(got_first_ref[k], got_second_ref[k], "gx") for k in range(3)
     )
     below, above = has_beside("gx")
     c_low, c_high = jnp.where(below, c_low, 0.0), jnp.where(above, c_high, 0.0)
@@ -175,7 +183,7 @@
     lines = images[1:-1] + [b_low] + [b_ref[i] for i in range(planes)] + [b_high, c_low]
     lines += [cond_ref[i] for i in range(planes)] + [c_high]
     for k, plane in enumerate(lines):
-        low, high = by_turn(plane[:1], plane[rows - 1 :], "gy")
+        low, high = to_send(plane[:1], plane[rows - 1 :], "gy")
         first_ref[k : k + 1] = low
         second_ref[k : k + 1] = high
 
@@ -218,7 +226,7 @@
     below, above = has_beside("gy")
     at_low = (index == 0) & below
     at_high = (index == rows - 1) & above
-    lines = by_turn(got_first_ref[...], got_second_ref[...], "gy")
+    lines = from_beside(got_first_ref[...], got_second_ref[...], "gy")
     images, beside = [], []
     for i in range(planes + 2):
         image = wide_ref[i]
@@ -299,18 +307,28 @@
 
 
 def swap(first, second, axis):
-    count = lax.axis_size(axis)
-    turns = []
-    for array, start in ((first, 0), (second, 1)):
-        pairs = [(i, (i + 1) % count) for i in range(start, count, 2)]
-        turns.append(lax.ppermute(array, axis, pairs + [(j, i) for i, j in pairs]))
-    return turns
+    count, across = lax.axis_size(axis), lax.axis_size(ACROSS[axis])
+
+    def number(place, line):
+        at = (place, line) if axis == "gx" else (line, place)
+        return at[0] * lax.axis_size("gy") + at[1]
+
+    pairs = []
+    for line in range(0, across, 2):
+        cycle = [number(i, line) for i in range(count)]
+        cycle += [number(i, line + 1) for i in reversed(range(count))]
+        pairs += list(zip(cycle, cycle[1:] + cycle[:1]))
+    back = [(j, i) for i, j in pairs]
+    return lax.ppermute(first, ("gx", "gy"), pairs), lax.ppermute(second, ("gx", "gy"), back)
 
 
 def everyones(sketch):
-    count = lax.axis_size("gx") * lax.axis_size("gy")
-    copies = jnp.broadcast_to(sketch[None], (count,) + sketch.shape)
-    return lax.all_to_all(copies, ("gx", "gy"), 0, 0)
+    nx, ny = lax.axis_size("gx"), lax.axis_size("gy")
+    pairs = [(i, i ^ 1) for i in range(nx)]
+    sketch = sketch + lax.ppermute(sketch, "gx", pairs)
+    groups = [[x * ny + y for x in range(turn, nx, 2) for y in range(ny)] for turn in range(2)]
+    copies = jnp.broadcast_to(sketch[None], (nx // 2 * ny,) + sketch.shape)
+    return lax.all_to_all(copies, ("gx", "gy"), 0, 0, axis_index_groups=groups)
 
 
 def body(b, warmth, phase, slots, draw):

time: 29.6 us -> 28.4 us (0.959)
  starting transfers between devices: 7.19 us -> 5.29 us
  waiting for transfers between devices: 6.03 us -> 7.09 us
  blocking collectives: 11 us -> 10.6 us
    ppermute x4 -> x5, starting transfers between devices: 7.19 us -> 5.29 us  [the longest x2 2.65 us: swap(): lax.ppermute(second, ('gx', 'gy'), back)]
    ppermute x4 -> x5, waiting for transfers between devices: 6.03 us -> 7.09 us  [the longest x2 3.98 us: swap(): lax.ppermute(first, ('gx', 'gy'), pairs)]
    all_to_all x1, blocking collectives: 11 us -> 10.6 us  [everyones(): return lax.all_to_all(copies, ('gx', 'gy'), 0, 0, axis_index_groups=groups)]
  transfers between devices with their start and end apart: 4 -> 5, of which waited for: 2 -> 4; matrix products, arithmetic and copies ran while one was open for 0% -> 0% of each run, Pallas kernels for 3% -> 3%
where the time goes in v1:
time: 28.4 us; the launch traced here: 28.3 us
  blocking collectives  10.6 us (37%)
  waiting for transfers between devices  7.09 us (25%)
  starting transfers between devices  5.29 us (19%)
  Pallas kernels  4.57 us (16%)
  between operations  0.66 us (2%)
    all_to_all x1, blocking collectives, everyones(): return lax.all_to_all(copies, ('gx', 'gy'), 0, 0, axis_index_groups=groups)  10.6 us
    pallas_call x5, Pallas kernels, call(): pl.pallas_call(kernel, out_shape=[jax.ShapeDtypeStruct(shape, jnp.float32...  4.57 us
    ppermute x2, waiting for transfers between devices, swap(): lax.ppermute(first, ('gx', 'gy'), pairs)  3.98 us
    ppermute x2, starting transfers between devices, swap(): lax.ppermute(second, ('gx', 'gy'), back)  2.65 us
    ppermute x2, starting transfers between devices, swap(): lax.ppermute(first, ('gx', 'gy'), pairs)  2.62 us
    ppermute x2, waiting for transfers between devices, swap(): lax.ppermute(second, ('gx', 'gy'), back)  1.97 us
    ppermute x1, waiting for transfers between devices, everyones(): sketch = sketch + lax.ppermute(sketch, 'gx', pairs)  1.14 us
  transfers between devices with their start and end apart: 5, of which 4 were waited for; matrix products, arithmetic and copies ran while one was open for 0% of the time, Pallas kernels for 3%

profile of v1, /device:TPU:0, one launch (start us, length us, event | category | flops | bytes accessed | tf_op | source)
XLA Modules:
  0.0 28.3 jit_solution(7226676936308321043)
XLA Ops:
  0.6 1.3 %shard_map.68 = (f32[4,8,1024]{2,1,0:T(8,128)S(1)}, f32[4,8,1024]{2,1,0:T(8,128)S(1)}, f32[4,8,1024]{2,1,0:T(8,128)S(1)}, f32[4,8,1024]{2,1,0:T(8,128)S(1)}, f32...) custom-call(f32[4,8,1024]{2,1,0:T(8,128)} %b_hbm.1, f32[4,8,1024]{2,1,0:T(8,128)} %warmth_hbm.1, s32[4,8,1024]{2,1,0:T(8,128)} %phase_hbm.1), custom_call_target="tpu_custom_call" | custom-call | tf_op jit(solution)/shard_map/pallas_call | solution.py:298
  1.9 0.5 %collective-permute-start = (f32[3,8,1024]{2,1,0:T(8,128)S(1)}, f32[3,8,1024]{2,1,0:T(8,128)S(1)}, u32[]{:S(2)}, u32[]{:S(2)}) collective-permute-start(f32[3,8,1024]{2,1,0:T(8,128)S(1)} %get-tuple-element.19), channel_id=1, source_target_pairs={{0,4},{4,8},{8,12},{12,13},{13,9},{9,5},{5,1},{1,0},{2,6},{6,10},{... | collective-permute-start | bytes 294920 | tf_op jit(solution)/shard_map/ppermute | solution.py:322
  2.5 2.6 %collective-permute-start.1 = (f32[3,8,1024]{2,1,0:T(8,128)S(1)}, f32[3,8,1024]{2,1,0:T(8,128)S(1)}, u32[]{:S(2)}, u32[]{:S(2)}) collective-permute-start(f32[3,8,1024]{2,1,0:T(8,128)S(1)} %get-tuple-element.20), channel_id=1, source_target_pairs={{4,0},{8,4},{12,8},{13,12},{9,13},{5,9},{1,5},{0,1},{6,2},{10,6},{... | collective-permute-start | bytes 294920 | tf_op jit(solution)/shard_map/ppermute | solution.py:322
  5.1 2.5 %collective-permute-done.got_first_ref = f32[3,8,1024]{2,1,0:T(8,128)S(1)} collective-permute-done((f32[3,8,1024]{2,1,0:T(8,128)S(1)}, f32[3,8,1024]{2,1,0:T(8,128)S(1)}, u32[]{:S(2)}, u32[]{:S(2)}) %collective-permute-start) | collective-permute-done | bytes 98336 | tf_op jit(solution)/shard_map/ppermute | solution.py:322
  7.6 0.0 collective-permute-done.1.got_second_ref
  7.6 0.0 copy-start
  7.6 0.0 copy-start.1
  7.6 0.2 shard_map.69
  7.8 2.1 %collective-permute-start.2 = (f32[16,1024]{1,0:T(8,128)S(1)}, f32[16,1024]{1,0:T(8,128)S(1)}, u32[]{:S(2)}, u32[]{:S(2)}) collective-permute-start(f32[16,1024]{1,0:T(8,128)S(1)} %get-tuple-element.23), channel_id=1, source_target_pairs={{0,1},{1,2},{2,3},{3,7},{7,6},{6,5},{5,4},{4,0},{8,9},{9,10},{10,1... | collective-permute-start | bytes 196616 | tf_op jit(solution)/shard_map/ppermute | solution.py:322
  9.9 0.0 collective-permute-start.3
  9.9 0.0 copy-done
  9.9 0.0 copy-done.1
  9.9 0.8 %shard_map.70.inside_ref = f32[8,128]{1,0:T(8,128)S(1)} custom-call(f32[4,8,1024]{2,1,0:T(8,128)S(1)} %get-tuple-element.15.b_ref, f32[4,8,1024]{2,1,0:T(8,128)S(1)} %get-tuple-element.16.cond_ref, f32[4,8,1024]{2,1,0:T(8,128)S(1)} %get-tuple-element.17.cap_ref, s32[4,8,1024]{2,1,0:T(8,128)S(1)} %copy-done, f32[4,8,1024]{2,1,0:T(8,128)S(1)} %copy-done.1, ...), custom_call_target="tpu_custom_call" | custom-call | flops 25165824 | tf_op jit(solution)/shard_map/pallas_call | solution.py:298
  10.8 1.5 %collective-permute-done.2.got_first_ref = f32[16,1024]{1,0:T(8,128)S(1)} collective-permute-done((f32[16,1024]{1,0:T(8,128)S(1)}, f32[16,1024]{1,0:T(8,128)S(1)}, u32[]{:S(2)}, u32[]{:S(2)}) %collective-permute-start.2) | collective-permute-done | bytes 65568 | tf_op jit(solution)/shard_map/ppermute | solution.py:322
  12.2 2.0 %collective-permute-done.3.got_second_ref = f32[16,1024]{1,0:T(8,128)S(1)} collective-permute-done((f32[16,1024]{1,0:T(8,128)S(1)}, f32[16,1024]{1,0:T(8,128)S(1)}, u32[]{:S(2)}, u32[]{:S(2)}) %collective-permute-start.3) | collective-permute-done | bytes 65568 | tf_op jit(solution)/shard_map/ppermute | solution.py:322
  14.2 1.0 %shard_map.71 = (f32[4,8,1024]{2,1,0:T(8,128)S(1)}, f32[4,8,1024]{2,1,0:T(8,128)S(1)}, f32[4,128]{1,0:T(4,128)S(1)}) custom-call(f32[4,8,1024]{2,1,0:T(8,128)S(1)} %get-tuple-element.15.b_ref, f32[4,8,1024]{2,1,0:T(8,128)S(1)} %get-tuple-element.16.cond_ref, f32[4,8,1024]{2,1,0:T(8,128)S(1)} %get-tuple-element.17.cap_ref, s32[4,8,1024]{2,1,0:T(8,128)S(1)} %copy-done, ...), custom_call_target="tpu_custom_call" | custom-call | flops 25165824 | tf_op jit(solution)/shard_map/pallas_call | solution.py:298
  15.2 0.0 collective-permute-start.4
  15.2 1.1 %collective-permute-done.4 = f32[4,128]{1,0:T(4,128)S(1)} collective-permute-done((f32[4,128]{1,0:T(4,128)S(1)}, f32[4,128]{1,0:T(4,128)S(1)}, u32[]{:S(2)}, u32[]{:S(2)}) %collective-permute-start.4) | collective-permute-done | bytes 2080 | tf_op jit(solution)/shard_map/ppermute | solution.py:328
  16.4 10.6 %all_to_all.5.sketch_ref = f32[8,4,128]{2,1,0:T(4,128)S(1)} all-to-all(f32[8,4,128]{2,1,0:T(4,128)S(1)} %broadcast_in_dim.2), channel_id=1, replica_groups={{0,1,2,3,8,9,10,11},{4,5,6,7,12,13,14,15},{16,17,18,19,24,25,26,27},{20..., dimensions={0} | all-to-all | bytes 32768 | tf_op jit(solution)/shard_map/all_to_all | solution.py:331
  27.0 1.2 %shard_map.72 = (f32[4,8,1024]{2,1,0:T(8,128)}, f32[4,8,1024]{2,1,0:T(8,128)}) custom-call(f32[8,4,128]{2,1,0:T(4,128)S(1)} %all_to_all.5.sketch_ref, f32[4,8,1024]{2,1,0:T(8,128)S(1)} %get-tuple-element.15.b_ref, f32[4,8,1024]{2,1,0:T(8,128)S(1)} %get-tuple-element.26.image_ref, f32[4,8,1024]{2,1,0:T(8,128)S(1)} %get-tuple-element.27.twice_ref), custom_call_target="tpu_custom_call" | custom-call | tf_op jit(solution)/shard_map/pallas_call | solution.py:298
  (2 shorter events, 0.0 us)
Async XLA Ops:
  1.9 5.7 %collective-permute-start = (f32[3,8,1024]{2,1,0:T(8,128)S(1)}, f32[3,8,1024]{2,1,0:T(8,128)S(1)}, u32[]{:S(2)}, u32[]{:S(2)}) collective-permute-start(f32[3,8,1024]{2,1,0:T(8,128)S(1)} %get-tuple-element.19), channel_id=1, source_target_pairs={{0,4},{4,8},{8,12},{12,13},{13,9},{9,5},{5,1},{1,0},{2,6},{6,10},{... | collective-permute-start | bytes 294920 | tf_op jit(solution)/shard_map/ppermute | solution.py:322
  2.5 5.2 %collective-permute-start.1 = (f32[3,8,1024]{2,1,0:T(8,128)S(1)}, f32[3,8,1024]{2,1,0:T(8,128)S(1)}, u32[]{:S(2)}, u32[]{:S(2)}) collective-permute-start(f32[3,8,1024]{2,1,0:T(8,128)S(1)} %get-tuple-element.20), channel_id=1, source_target_pairs={{4,0},{8,4},{12,8},{13,12},{9,13},{5,9},{1,5},{0,1},{6,2},{10,6},{... | collective-permute-start | bytes 294920 | tf_op jit(solution)/shard_map/ppermute | solution.py:322
  7.6 2.3 %copy-start = (s32[4,8,1024]{2,1,0:T(8,128)S(1)}, s32[4,8,1024]{2,1,0:T(8,128)}, u32[]{:S(2)}) copy-start(s32[4,8,1024]{2,1,0:T(8,128)} %slot_ref.3) | copy-start | bytes 393220
  7.6 2.3 %copy-start.1 = (f32[4,8,1024]{2,1,0:T(8,128)S(1)}, f32[4,8,1024]{2,1,0:T(8,128)}, u32[]{:S(2)}) copy-start(f32[4,8,1024]{2,1,0:T(8,128)} %draw_ref.3) | copy-start | bytes 393220
  7.8 4.4 %collective-permute-start.2 = (f32[16,1024]{1,0:T(8,128)S(1)}, f32[16,1024]{1,0:T(8,128)S(1)}, u32[]{:S(2)}, u32[]{:S(2)}) collective-permute-start(f32[16,1024]{1,0:T(8,128)S(1)} %get-tuple-element.23), channel_id=1, source_target_pairs={{0,1},{1,2},{2,3},{3,7},{7,6},{6,5},{5,4},{4,0},{8,9},{9,10},{10,1... | collective-permute-start | bytes 196616 | tf_op jit(solution)/shard_map/ppermute | solution.py:322
  9.9 4.3 %collective-permute-start.3 = (f32[16,1024]{1,0:T(8,128)S(1)}, f32[16,1024]{1,0:T(8,128)S(1)}, u32[]{:S(2)}, u32[]{:S(2)}) collective-permute-start(f32[16,1024]{1,0:T(8,128)S(1)} %get-tuple-element.24), channel_id=1, source_target_pairs={{1,0},{2,1},{3,2},{7,3},{6,7},{5,6},{4,5},{0,4},{9,8},{10,9},{11,1... | collective-permute-start | bytes 196616 | tf_op jit(solution)/shard_map/ppermute | solution.py:322
  15.2 1.2 %collective-permute-start.4 = (f32[4,128]{1,0:T(4,128)S(1)}, f32[4,128]{1,0:T(4,128)S(1)}, u32[]{:S(2)}, u32[]{:S(2)}) collective-permute-start(f32[4,128]{1,0:T(4,128)S(1)} %get-tuple-element.25), channel_id=1, source_target_pairs={{0,4},{4,0},{8,12},{12,8},{1,5},{5,1},{9,13},{13,9},{2,6},{6,2},{1... | collective-permute-start | bytes 6152 | tf_op jit(solution)/shard_map/ppermute | solution.py:328
